TPU v7x, 256 devices: a whole 4x4x8 slice. The times are simulated.
256 devices in a mesh: wide: 64 (over y, z, core), orb: 4 (over x).
Axes of the slice: x: 4, y: 4, z: 8, core: 2. Of those that a mesh axis runs over, the one named last changes fastest.
Arguments:
- green_packed: bfloat16 [2, 64, 16, 256, 256], P(None, 'wide', 'orb'), may hold values from -6 to 6
- bubble_weight: float32 [16, 16], replicated, may hold values from -1.5 to 1.5
- tile_owner: int32 [64], replicated, may hold values from 0 to 63, as said below
- pairing: int32 [64], replicated, may hold values from 0 to 63, as said below
Outputs:
- response: bfloat16 [2, 64, 16, 256, 256], P(None, 'wide', 'orb')
Inputs may be any that keep to these rules, and one draw needn't show every extreme that they name: `tile_owner`: A permutation of the 64 time tiles; slot s lies on index s // (8 * 8 / 64) of wide. The tiles in slots s and s + 32 are mirror images (tiles i * 8 + j and j * 8 + i) or both diagonal tiles. pairing[s] is the slot whose tile is the mirror image of tile_owner[s]: s itself for a diagonal tile, else the slot 32 away.
All inputs are finite; a program needn't handle non-finite values.
Results may differ from a plain program's by a relative error of at most 0.018.
Values may be sent and summed in bfloat16 or wider, within the bound.
A program may use at most 128 MiB of HBM per device.

v0:
```python
import math

import jax
import jax.numpy as jnp
from jax import lax
from jax.experimental import pallas as pl
from jax.experimental.pallas import tpu as pltpu
from jax.sharding import PartitionSpec as P

NORB = 4
NT = 256
K = 64
HALF = 128
NDEV = 256

f32 = jnp.float32
bf16 = jnp.bfloat16


def shear(x, h):
    lane = lax.broadcasted_iota(jnp.int32, (NT, HALF), 1)
    if h:
        x = jnp.concatenate([x[HALF:], x[:HALF]], axis=0)
    for bit in (6, 5, 4, 3):
        m = 1 << bit
        y = x.reshape(NT // (2 * m), 2, m, HALF)
        swapped = jnp.concatenate([y[:, 1:2], y[:, 0:1]], axis=1).reshape(NT, HALF)
        x = jnp.where((lane & m) != 0, swapped, x)
    lane = lax.broadcasted_iota(jnp.int32, (NT // 8, 8, HALF), 2)
    row = lax.broadcasted_iota(jnp.int32, (NT // 8, 8, HALF), 1)
    x = x.reshape(NT // 8, 8, HALF)
    for bit in (2, 1, 0):
        m = 1 << bit
        swapped = pltpu.roll(x, m, 1)
        if bit < 2:
            swapped = jnp.where((row & m) != 0, swapped, pltpu.roll(x, 8 - m, 1))
        x = jnp.where((lane & m) != 0, swapped, x)
    return x.reshape(NT, HALF)


def add(u, v):
    return (u[0] + v[0], u[1] + v[1])


def sub(u, v):
    return (u[0] - v[0], u[1] - v[1])


def times(u, cr, ci):
    return (u[0] * cr - u[1] * ci, u[0] * ci + u[1] * cr)


def turn(u, sign):
    return (-u[1], u[0]) if sign > 0 else (u[1], -u[0])


def fft4(a, b, c, d, sign):
    t0, t1, t2, t3 = add(a, c), sub(a, c), add(b, d), turn(sub(b, d), sign)
    return [add(t0, t2), add(t1, t3), sub(t0, t2), sub(t1, t3)]


def fft8(x, sign):
    even = fft4(x[0], x[2], x[4], x[6], sign)
    odd = fft4(x[1], x[3], x[5], x[7], sign)
    c = math.sqrt(0.5)
    odd = [
        odd[0],
        ((odd[1][0] - sign * odd[1][1]) * c, (sign * odd[1][0] + odd[1][1]) * c),
        turn(odd[2], sign),
        ((-odd[3][0] - sign * odd[3][1]) * c, (sign * odd[3][0] - odd[3][1]) * c),
    ]
    return [add(e, o) for e, o in zip(even, odd)] + [sub(e, o) for e, o in zip(even, odd)]


def fft64(load, store, mid, sign):
    for k2 in range(8):
        y = fft8([load(8 * k1 + k2) for k1 in range(8)], sign)
        for r1 in range(8):
            v = y[r1]
            angle = 2.0 * math.pi * k2 * r1 / 64
            cr, ci = 0.125 * math.cos(angle), sign * 0.125 * math.sin(angle)
            v = times(v, cr, ci) if k2 * r1 else (v[0] * 0.125, v[1] * 0.125)
            mid[0, r1 * 8 + k2] = v[0]
            mid[1, r1 * 8 + k2] = v[1]
    for r1 in range(8):
        y = fft8([(mid[0, r1 * 8 + k2], mid[1, r1 * 8 + k2]) for k2 in range(8)], sign)
        for r2 in range(8):
            store(r1 + 8 * r2, y[r2])


def both_parts(tile):
    x = tile.astype(f32)
    return (x[:8], x[8:])


def tile_of(v):
    return jnp.concatenate([v[0], v[1]], axis=0).astype(bf16)


def kernel(
    x_ref, w_ref, o_ref, rows, snd, rcv, mid, rg, mir, self_real, wv, snd2, rcv2, g, rhs_r, rhs_la, lhs, s1, r1, s2, r2, s3, r3, s4
):
    orb = lax.axis_index("orb")
    wide = lax.axis_index("wide")
    me = wide * NORB + orb

    def place(d):
        return (d // NORB, d % NORB)

    def shear_plane(p, carry):
        c, b = p // 4, p % 4
        for h in range(2):
            x = x_ref[p, :, h * HALF : (h + 1) * HALF].astype(f32)
            rows[pl.ds(pl.multiple_of((c * 8 + h * 4 + b) * NT, NT), NT), :] = shear(x, h)
        return carry

    lax.fori_loop(0, 8, shear_plane, 0)

    def make_tile(e):
        snd[e] = tile_of((rows[pl.ds(e, 8, stride=NT), :], rows[pl.ds(8 * NT + e, 8, stride=NT), :]))

    def send(i, carry):
        d = (me + i) % NDEV
        make_tile(d)
        pltpu.make_async_remote_copy(snd.at[d], rcv.at[me], s1, r1, device_id=place(d)).start()
        return carry

    lax.fori_loop(1, NDEV, send, 0)
    make_tile(me)
    rcv[me] = snd[me]

    for i in range(1, NORB):
        pltpu.make_async_remote_copy(x_ref, g.at[orb], s2, r2, device_id=(wide, (orb + i) % NORB)).start()
    own = pltpu.make_async_copy(x_ref, g.at[orb], s4)
    own.start()

    sub8 = lax.broadcasted_iota(jnp.int32, (8, HALF), 0) % 4
    for a2 in range(4):
        for a in range(4):
            for j in range(4):
                v = jnp.full((8, HALF), w_ref[a2 * 4, a * 4 + j], f32)
                for b2 in range(1, 4):
                    v = jnp.where(sub8 == b2, w_ref[a2 * 4 + b2, a * 4 + (b2 + j) % 4], v)
                wv[(a2 * 4 + a) * 4 + j] = v

    arrived = pltpu.make_async_remote_copy(snd.at[pl.ds(0, NDEV - 1)], rcv.at[pl.ds(0, NDEV - 1)], s1, r1, device_id=(wide, orb))
    arrived.wait_recv()

    def to_sites(a, carry):
        def store(r, v):
            rg[r * NORB + a] = tile_of(v)

        fft64(lambda k: both_parts(rcv[k * NORB + a]), store, mid, 1)
        return carry

    lax.fori_loop(0, NORB, to_sites, 0)

    low = me % HALF
    i0 = lax.broadcasted_iota(jnp.int32, (HALF, HALF), 0)
    i1 = lax.broadcasted_iota(jnp.int32, (HALF, HALF), 1)
    perm = jnp.where(i0 == (i1 ^ low), 1.0, 0.0).astype(bf16)

    def mirror_rows(i, carry):
        block = rg[pl.ds(i * 32, 32)].reshape(512, HALF)
        out = jnp.dot(block, perm, preferred_element_type=f32)
        mir[pl.ds(i * 32, 32)] = out.astype(bf16).reshape(32, 16, HALF)
        return carry

    lax.fori_loop(0, 8, mirror_rows, 0)

    swap = (lax.broadcasted_iota(jnp.int32, (8, HALF), 0) * 0 + me // HALF) == 1

    def site(r, carry):
        back = (K - r) % K
        own_v, shifted = [], []
        for a in range(4):
            u = both_parts(rg[r * NORB + a])
            v = both_parts(mir[back * NORB + a])
            v = tuple(jnp.where(swap, pltpu.roll(z, 4, 0), z) for z in v)
            own_v.append(u)
            prod = (u[0] * v[0] - u[1] * v[1], u[0] * v[1] + u[1] * v[0])
            turned = [prod]
            for j in (1, 2, 3):
                turned.append(tuple(jnp.where(sub8 < 4 - j, pltpu.roll(z, 8 - j, 0), pltpu.roll(z, 4 - j, 0)) for z in prod))
            shifted.append(turned)
        for a2 in range(4):
            re = im = None
            for a in range(4):
                for j in range(4):
                    w = wv[(a2 * 4 + a) * 4 + j]
                    tr, ti = w * shifted[a][j][0], w * shifted[a][j][1]
                    re = tr if re is None else re + tr
                    im = ti if im is None else im + ti
            u = own_v[a2]
            self_real[0, r * NORB + a2] = u[0] * re - u[1] * im
            self_real[1, r * NORB + a2] = u[0] * im + u[1] * re
        return carry

    lax.fori_loop(0, K, site, 0)

    def to_momenta(i, carry):
        a = (orb + i) % NORB

        def store(k, v):
            snd2[k * NORB + a] = tile_of(v)

        fft64(lambda r: (self_real[0, r * NORB + a], self_real[1, r * NORB + a]), store, mid, -1)

        def send_back(n, carry):
            k = (wide + n) % K
            d = k * NORB + a

            @pl.when(d != me)
            def _():
                pltpu.make_async_remote_copy(snd2.at[d], rcv2.at[me], s3, r3, device_id=(k, a)).start()

            return carry

        lax.fori_loop(0, K, send_back, 0)
        return carry

    lax.fori_loop(0, NORB, to_momenta, 0)
    rcv2[me] = snd2[me]

    own.wait()
    gathered = pltpu.make_async_remote_copy(g.at[pl.ds(0, 3)], g.at[pl.ds(0, 3)], s2, r2, device_id=(wide, orb))
    gathered.wait_recv()
    ti = lax.broadcasted_iota(jnp.int32, (NT, NT), 0)
    ui = lax.broadcasted_iota(jnp.int32, (NT, NT), 1)

    def operands(i, carry):
        c, b = i // 4, i % 4
        for part in range(2):
            own_g = g[c, part * 4 + b].astype(f32)
            adjoint = g[b, part * 4 + c].astype(f32).T
            if part:
                adjoint = -adjoint
            n = c * 2 + part
            rhs_r[b, n] = jnp.where(ti >= ui, own_g, 0.0).astype(bf16)
            rhs_la[b, n] = jnp.where(ti < ui, own_g, jnp.where(ti > ui, -adjoint, 0.0)).astype(bf16)
            rhs_la[b, 8 + n] = jnp.where(ti <= ui, adjoint, 0.0).astype(bf16)
        return carry

    lax.fori_loop(0, 16, operands, 0)

    returned = pltpu.make_async_remote_copy(snd2.at[pl.ds(0, NDEV - 1)], rcv2.at[pl.ds(0, NDEV - 1)], s3, r3, device_id=(wide, orb))
    returned.wait_recv()

    def spread(e, carry):
        re, im = both_parts(rcv2[e])
        rows[pl.ds(e, 8, stride=NT), :] = re
        rows[pl.ds(8 * NT + e, 8, stride=NT), :] = im
        return carry

    lax.fori_loop(0, NDEV, spread, 0)

    def left(c, carry):
        for h in range(2):
            t_pos = lax.broadcasted_iota(jnp.int32, (NT, HALF), 0)
            s_pos = lax.broadcasted_iota(jnp.int32, (NT, HALF), 1) + h * HALF
            lower = t_pos >= s_pos
            for part in range(2):
                x = shear(rows[pl.ds(pl.multiple_of((part * 8 + h * 4 + c) * NT, NT), NT), :], h)
                ret = jnp.where(lower, x, 0.0)
                les = jnp.where(lower, 0.0, x)
                for off, z in ((0, ret), (8, les)):
                    same = pl.multiple_of((off + c * 2 + part) * NT, NT) + h * HALF
                    other = pl.multiple_of((off + c * 2 + 1 - part) * NT, NT) + h * HALF
                    if part == 0:
                        lhs[:NT, pl.ds(same, HALF)] = z.astype(bf16)
                        lhs[NT:, pl.ds(other, HALF)] = z.astype(bf16)
                    else:
                        lhs[:NT, pl.ds(same, HALF)] = (-z).astype(bf16)
                        lhs[NT:, pl.ds(other, HALF)] = z.astype(bf16)
        return carry

    lax.fori_loop(0, NORB, left, 0)

    def products(b, carry):
        ret = jnp.dot(lhs[:, : 8 * NT], rhs_r[b].reshape(8 * NT, NT), preferred_element_type=f32)
        les = jnp.dot(lhs[...], rhs_la[b].reshape(16 * NT, NT), preferred_element_type=f32)
        for part in range(2):
            sl = slice(part * NT, (part + 1) * NT)
            o_ref[part * 4 + b] = (jnp.where(ti >= ui, ret[sl], les[sl]) * NT ** (-0.5)).astype(bf16)
        return carry

    lax.fori_loop(0, NORB, products, 0)

    arrived.wait_send()
    gathered.wait_send()
    returned.wait_send()


def local(green_packed, bubble_weight, tile_owner, pairing):
    planes = green_packed.reshape(8, NT, NT)
    vmem = pl.BlockSpec(memory_space=pltpu.VMEM)
    dma = pltpu.SemaphoreType.DMA
    out = pl.pallas_call(
        kernel,
        out_shape=jax.ShapeDtypeStruct((8, NT, NT), bf16),
        in_specs=[vmem, pl.BlockSpec(memory_space=pltpu.SMEM)],
        out_specs=vmem,
        scratch_shapes=[
            pltpu.VMEM((16 * NT, HALF), f32),
            pltpu.VMEM((NDEV, 16, HALF), bf16),
            pltpu.VMEM((NDEV, 16, HALF), bf16),
            pltpu.VMEM((2, K, 8, HALF), f32),
            pltpu.VMEM((NDEV, 16, HALF), bf16),
            pltpu.VMEM((NDEV, 16, HALF), bf16),
            pltpu.VMEM((2, NDEV, 8, HALF), f32),
            pltpu.VMEM((64, 8, HALF), f32),
            pltpu.VMEM((NDEV, 16, HALF), bf16),
            pltpu.VMEM((NDEV, 16, HALF), bf16),
            pltpu.VMEM((NORB, 8, NT, NT), bf16),
            pltpu.VMEM((NORB, 8, NT, NT), bf16),
            pltpu.VMEM((NORB, 16, NT, NT), bf16),
            pltpu.VMEM((2 * NT, 16 * NT), bf16),
        ]
        + [dma] * 7,
        compiler_params=pltpu.CompilerParams(has_side_effects=True, vmem_limit_bytes=56 << 20),
        cost_estimate=pl.CostEstimate(flops=7 * 10**9, bytes_accessed=2 << 20, transcendentals=0),
    )(planes, bubble_weight)
    return out.reshape(green_packed.shape)


def solution(mesh):
    return jax.shard_map(
        local,
        mesh=mesh,
        in_specs=(P(None, "wide", "orb", None, None), P(), P(), P()),
        out_specs=P(None, "wide", "orb", None, None),
        check_vma=False,
    )
```

profile of v0, /device:TPU:1, one launch (start us, length us, event | category | flops | bytes accessed | tf_op | source)
XLA Modules:
  0.0 107.8 jit_solution(12942442693314427506)
XLA Ops:
  0.0 105.5 %shard_map.28 = bf16[8,256,256]{2,1,0:T(8,128)(2,1)} custom-call(bf16[8,256,256]{2,1,0:T(8,128)(2,1)} %bitcast.5, f32[16,16]{1,0:T(8,128)} %w_ref.1), custom_call_target="tpu_custom_call" | custom-call | flops 7000000000 | bytes 2097152 | tf_op jit(solution)/shard_map/pallas_call | solution.py:298
  105.6 2.3 %copy.5 = bf16[2,1,4,256,256]{4,3,2,1,0:T(8,128)(2,1)} copy(bf16[2,1,4,256,256]{4,3,2,1,0:T(8,128)(2,1)} %bitcast.4) | data formatting | bytes 2097152
where the time goes:
time: 108 us
  Pallas kernels  106 us (98%)
  local copies, waits for them, and re-layouts  2.26 us (2%)
    pallas_call x1, Pallas kernels, local(): pl.pallas_call(kernel, out_shape=jax.ShapeDtypeStruct((8, NT, NT), bf16),...  106 us
    unnamed x1, local copies, waits for them, and re-layouts  2.26 us

commit v1 on v0

v1 whole, which is shorter than its diff:
```python
import math

import jax
import jax.numpy as jnp
from jax import lax
from jax.experimental import pallas as pl
from jax.experimental.pallas import tpu as pltpu
from jax.sharding import PartitionSpec as P

NORB = 4
NT = 256
K = 64
HALF = 128
NDEV = 256

f32 = jnp.float32
bf16 = jnp.bfloat16

R00, R11, R10, L00, L11, L01, A00, A11, A01 = range(9)


def shear(x, h):
    lane = lax.broadcasted_iota(jnp.int32, (NT, HALF), 1)
    if h:
        x = jnp.concatenate([x[HALF:], x[:HALF]], axis=0)
    for bit in (6, 5, 4, 3):
        m = 1 << bit
        y = x.reshape(NT // (2 * m), 2, m, HALF)
        swapped = jnp.concatenate([y[:, 1:2], y[:, 0:1]], axis=1).reshape(NT, HALF)
        x = jnp.where((lane & m) != 0, swapped, x)
    lane = lax.broadcasted_iota(jnp.int32, (NT // 8, 8, HALF), 2)
    row = lax.broadcasted_iota(jnp.int32, (NT // 8, 8, HALF), 1)
    x = x.reshape(NT // 8, 8, HALF)
    for bit in (2, 1, 0):
        m = 1 << bit
        swapped = pltpu.roll(x, m, 1)
        if bit < 2:
            swapped = jnp.where((row & m) != 0, swapped, pltpu.roll(x, 8 - m, 1))
        x = jnp.where((lane & m) != 0, swapped, x)
    return x.reshape(NT, HALF)


def add(u, v):
    return (u[0] + v[0], u[1] + v[1])


def sub(u, v):
    return (u[0] - v[0], u[1] - v[1])


def times(u, cr, ci):
    return (u[0] * cr - u[1] * ci, u[0] * ci + u[1] * cr)


def turn(u, sign):
    return (-u[1], u[0]) if sign > 0 else (u[1], -u[0])


def fft4(a, b, c, d, sign):
    t0, t1, t2, t3 = add(a, c), sub(a, c), add(b, d), turn(sub(b, d), sign)
    return [add(t0, t2), add(t1, t3), sub(t0, t2), sub(t1, t3)]


def fft8(x, sign):
    even = fft4(x[0], x[2], x[4], x[6], sign)
    odd = fft4(x[1], x[3], x[5], x[7], sign)
    c = math.sqrt(0.5)
    odd = [
        odd[0],
        ((odd[1][0] - sign * odd[1][1]) * c, (sign * odd[1][0] + odd[1][1]) * c),
        turn(odd[2], sign),
        ((-odd[3][0] - sign * odd[3][1]) * c, (sign * odd[3][0] - odd[3][1]) * c),
    ]
    return [add(e, o) for e, o in zip(even, odd)] + [sub(e, o) for e, o in zip(even, odd)]


def fft64(load, store, mid, sign):
    for k2 in range(8):
        y = fft8([load(8 * k1 + k2) for k1 in range(8)], sign)
        for r1 in range(8):
            v = y[r1]
            angle = 2.0 * math.pi * k2 * r1 / 64
            cr, ci = 0.125 * math.cos(angle), sign * 0.125 * math.sin(angle)
            v = times(v, cr, ci) if k2 * r1 else (v[0] * 0.125, v[1] * 0.125)
            mid[0, r1 * 8 + k2] = v[0]
            mid[1, r1 * 8 + k2] = v[1]
    for r1 in range(8):
        y = fft8([(mid[0, r1 * 8 + k2], mid[1, r1 * 8 + k2]) for k2 in range(8)], sign)
        for r2 in range(8):
            store(r1 + 8 * r2, y[r2])


def both_parts(tile):
    x = tile.astype(f32)
    return (x[:8], x[8:])


def tile_of(v):
    return jnp.concatenate([v[0], v[1]], axis=0).astype(bf16)


def kernel(
    x_ref, w_ref, o_ref, rows, snd, rcv, mid, rg, mir, self_real, wv, snd2, rcv2, g, rhs, lhs, s1, r1, s2, r2, s3, r3, s4
):
    orb = lax.axis_index("orb")
    wide = lax.axis_index("wide")
    me = wide * NORB + orb

    def place(d):
        return (d // NORB, d % NORB)

    barrier = pltpu.get_barrier_semaphore()

    def greet(i, carry):
        pl.semaphore_signal(barrier, inc=1, device_id=place((me + i) % NDEV), device_id_type=pl.DeviceIdType.MESH)
        return carry

    lax.fori_loop(1, NDEV, greet, 0)

    def shear_plane(p, carry):
        c, b = p // 4, p % 4
        for h in range(2):
            x = x_ref[p, :, h * HALF : (h + 1) * HALF].astype(f32)
            rows[pl.ds(pl.multiple_of((c * 8 + h * 4 + b) * NT, NT), NT), :] = shear(x, h)
        return carry

    lax.fori_loop(0, 8, shear_plane, 0)

    def make_tile(e):
        snd[e] = tile_of((rows[pl.ds(e, 8, stride=NT), :], rows[pl.ds(8 * NT + e, 8, stride=NT), :]))

    def pack(i, carry):
        for n in range(4):
            make_tile(i * 4 + n)
        return carry

    lax.fori_loop(0, NDEV // 4, pack, 0)
    rcv[orb, wide] = snd[me]
    pl.semaphore_wait(barrier, NDEV - 1)

    def send(i, carry):
        step, n = i // K, i % K
        there = (wide + n) % K
        plane = (orb + step) % NORB
        d = there * NORB + plane
        pltpu.make_async_remote_copy(snd.at[d], rcv.at[orb, wide], s1.at[step], r1.at[step], device_id=(there, plane)).start()
        return carry

    lax.fori_loop(1, NDEV, send, 0)

    right, left_ = (orb + 1) % NORB, (orb + 3) % NORB
    hops = [
        pltpu.make_async_remote_copy(x_ref, g.at[orb], s2.at[0], r2.at[0], device_id=(wide, right)),
        pltpu.make_async_remote_copy(x_ref, g.at[orb], s2.at[1], r2.at[1], device_id=(wide, left_)),
    ]
    for hop in hops:
        hop.start()
    own = pltpu.make_async_copy(x_ref, g.at[orb], s4)
    own.start()

    q_of = lax.broadcasted_iota(jnp.int32, (HALF, 16), 0)
    pick = (q_of % 32 // 8 * 4 + q_of % 4 == lax.broadcasted_iota(jnp.int32, (HALF, 16), 1)).astype(bf16)
    i0 = lax.broadcasted_iota(jnp.int32, (HALF, HALF), 0)
    i1 = lax.broadcasted_iota(jnp.int32, (HALF, HALF), 1)
    same = (i0 // 32 == i1 // 32) & (i0 % 8 // 4 == i1 % 8 // 4)
    weight = w_ref[...]
    high = weight.astype(bf16)
    wide_w = []
    for part in (high, (weight - high.astype(f32)).astype(bf16)):
        z = jnp.dot(pick, part, preferred_element_type=f32).astype(bf16)
        z = lax.dot_general(z, pick, (((1,), (1,)), ((), ())), preferred_element_type=f32)
        wide_w.append(jnp.where(same, z, 0.0).astype(bf16))
    wv[...] = jnp.concatenate([wide_w[0], wide_w[1], wide_w[0]], axis=1)

    arrived = []
    for step in range(NORB):
        a = (orb + NORB - step) % NORB
        count = K - 1 if step == 0 else K
        block = rcv.at[0, pl.ds(0, count)]
        arrived.append(pltpu.make_async_remote_copy(block, block, s1.at[step], r1.at[step], device_id=(wide, orb)))
        arrived[step].wait_recv()

        def store(r, v):
            rg[r * NORB + a] = tile_of(v)

        fft64(lambda k: both_parts(rcv[a, k]), store, mid, 1)

    for hop in hops:
        hop.wait_recv()
    more = [
        pltpu.make_async_remote_copy(g.at[left_, pl.ds(0, 4)], g.at[left_, pl.ds(0, 4)], s2.at[2], r2.at[2], device_id=(wide, right)),
        pltpu.make_async_remote_copy(g.at[right, pl.ds(4, 4)], g.at[right, pl.ds(4, 4)], s2.at[3], r2.at[3], device_id=(wide, left_)),
    ]
    for hop in more:
        hop.start()

    low = me % HALF
    perm = jnp.where(i0 == (i1 ^ low), 1.0, 0.0).astype(bf16)

    def mirror_rows(i, carry):
        block = rg[pl.ds(i * 32, 32)].reshape(512, HALF)
        out = jnp.dot(block, perm, preferred_element_type=f32)
        mir[pl.ds(i * 32, 32)] = out.astype(bf16).reshape(32, 16, HALF)
        return carry

    lax.fori_loop(0, 8, mirror_rows, 0)

    swap = (lax.broadcasted_iota(jnp.int32, (8, HALF), 0) * 0 + me // HALF) == 1

    def sites(i, carry):
        prod_re, prod_im = [], []
        for n in range(4):
            r = i * 4 + n
            back = (K - r) % K
            for a in range(4):
                u = both_parts(rg[r * NORB + a])
                v = both_parts(mir[back * NORB + a])
                v = tuple(jnp.where(swap, pltpu.roll(z, 4, 0), z) for z in v)
                prod_re.append(u[0] * v[0] - u[1] * v[1])
                prod_im.append(u[0] * v[1] + u[1] * v[0])
        prod = jnp.concatenate([jnp.concatenate(prod_re, axis=0), jnp.concatenate(prod_im, axis=0)], axis=1)
        high = prod.astype(bf16)
        rest = (prod - high.astype(f32)).astype(bf16)
        bubble = jnp.dot(wv[...], jnp.concatenate([high, high, rest], axis=0), preferred_element_type=f32)
        for n in range(4):
            r = i * 4 + n
            for a in range(4):
                row = (n * 4 + a) * 8
                re, im = bubble[row : row + 8, :HALF], bubble[row : row + 8, HALF:]
                u = both_parts(rg[r * NORB + a])
                self_real[0, r * NORB + a] = u[0] * re - u[1] * im
                self_real[1, r * NORB + a] = u[0] * im + u[1] * re
        return carry

    lax.fori_loop(0, K // 4, sites, 0)

    for step in range(NORB):
        a = (orb + step) % NORB

        def store(k, v):
            snd2[k * NORB + a] = tile_of(v)

        fft64(lambda r: (self_real[0, r * NORB + a], self_real[1, r * NORB + a]), store, mid, -1)

        def send_back(n, carry):
            k = (wide + n) % K
            pltpu.make_async_remote_copy(
                snd2.at[k * NORB + a], rcv2.at[orb, wide], s3.at[step], r3.at[step], device_id=(k, a)
            ).start()
            return carry

        lax.fori_loop(1 if step == 0 else 0, K, send_back, 0)
    rcv2[orb, wide] = snd2[me]

    own.wait()
    for hop in more:
        hop.wait_recv()
    ge, gt = i0 >= i1, i0 > i1

    def operands(i, carry):
        c, bp = i // 2, i % 2
        for half in range(2):
            b = bp * 2 + half
            lanes = slice(half * HALF, (half + 1) * HALF)
            for part in range(2):
                m = pl.ds(pl.multiple_of((c * 2 + part) * HALF, HALF), HALF)
                own_g = g[c, part * 4 + b].astype(f32)
                adjoint = g[b, part * 4 + c].astype(f32).T
                if part:
                    adjoint = -adjoint
                for n in range(2):
                    blk = slice(n * HALF, (n + 1) * HALF)
                    x, y = own_g[blk, blk], adjoint[blk, blk]
                    rhs[R00 + n, bp, m, lanes] = jnp.where(ge, x, 0.0).astype(bf16)
                    rhs[L00 + n, bp, m, lanes] = jnp.where(ge, jnp.where(gt, -y, 0.0), x).astype(bf16)
                    rhs[A00 + n, bp, m, lanes] = jnp.where(gt, 0.0, y).astype(bf16)
                rhs[R10, bp, m, lanes] = own_g[HALF:, :HALF].astype(bf16)
                rhs[L01, bp, m, lanes] = own_g[:HALF, HALF:].astype(bf16)
                rhs[A01, bp, m, lanes] = adjoint[:HALF, HALF:].astype(bf16)
        return carry

    lax.fori_loop(0, 8, operands, 0)

    returned = []
    for step in range(NORB):
        count = K - 1 if step == 0 else K
        block = rcv2.at[0, pl.ds(0, count)]
        returned.append(pltpu.make_async_remote_copy(block, block, s3.at[step], r3.at[step], device_id=(wide, orb)))
        returned[step].wait_recv()
        plane = (orb + NORB - step) % NORB

        def spread(i, carry):
            for n in range(4):
                w = i * 4 + n
                e = w * NORB + plane
                re, im = both_parts(rcv2[plane, w])
                rows[pl.ds(e, 8, stride=NT), :] = re
                rows[pl.ds(8 * NT + e, 8, stride=NT), :] = im
            return carry

        lax.fori_loop(0, K // 4, spread, 0)

    def left(c, carry):
        for h in range(2):
            for part in range(2):
                x = shear(rows[pl.ds(pl.multiple_of((part * 8 + h * 4 + c) * NT, NT), NT), :], h)
                top, low_half = x[:HALF], x[HALF:]
                if h == 0:
                    placed = ((0, 0, jnp.where(ge, top, 0.0)), (0, 1, jnp.where(ge, 0.0, top)), (1, 0, low_half))
                else:
                    placed = ((0, 2, top), (1, 1, jnp.where(ge, low_half, 0.0)), (1, 2, jnp.where(ge, 0.0, low_half)))
                for t, n, z in placed:
                    same = pl.multiple_of(n * 8 * HALF + (c * 2 + part) * HALF, HALF)
                    other = pl.multiple_of(n * 8 * HALF + (c * 2 + 1 - part) * HALF, HALF)
                    lhs[t, :HALF, pl.ds(same, HALF)] = (-z if part else z).astype(bf16)
                    lhs[t, HALF:, pl.ds(other, HALF)] = z.astype(bf16)
        return carry

    lax.fori_loop(0, NORB, left, 0)

    def products(bp, carry):
        def dot(t, first, *blocks):
            z = lhs[t, :, first * 8 * HALF : (first + len(blocks)) * 8 * HALF]
            return jnp.dot(z, jnp.concatenate([rhs[n, bp] for n in blocks], axis=0), preferred_element_type=f32)

        mask = jnp.concatenate([jnp.concatenate([ge, ge], axis=0)] * 2, axis=1)
        quarters = {
            (0, 0): jnp.where(mask, dot(0, 0, R00), dot(0, 0, L00, A00)),
            (0, 1): dot(0, 0, L01, A01, A11),
            (1, 0): dot(1, 0, R00, R10),
            (1, 1): jnp.where(mask, dot(1, 1, R11), dot(1, 0, L01, L11, A11)),
        }
        for (t, u), z in quarters.items():
            z = (z * NT ** (-0.5)).astype(bf16)
            for part in range(2):
                for half in range(2):
                    o_ref[part * 4 + bp * 2 + half, t * HALF : (t + 1) * HALF, u * HALF : (u + 1) * HALF] = z[
                        part * HALF : (part + 1) * HALF, half * HALF : (half + 1) * HALF
                    ]
        return carry

    lax.fori_loop(0, 2, products, 0)

    for copy in arrived + hops + more + returned:
        copy.wait_send()


def local(green_packed, bubble_weight, tile_owner, pairing):
    planes = green_packed.reshape(8, NT, NT)
    vmem = pl.BlockSpec(memory_space=pltpu.VMEM)
    dma = pltpu.SemaphoreType.DMA
    out = pl.pallas_call(
        kernel,
        out_shape=jax.ShapeDtypeStruct((8, NT, NT), bf16),
        in_specs=[vmem, vmem],
        out_specs=vmem,
        scratch_shapes=[
            pltpu.VMEM((16 * NT, HALF), f32),
            pltpu.VMEM((NDEV, 16, HALF), bf16),
            pltpu.VMEM((NORB, K, 16, HALF), bf16),
            pltpu.VMEM((2, K, 8, HALF), f32),
            pltpu.VMEM((NDEV, 16, HALF), bf16),
            pltpu.VMEM((NDEV, 16, HALF), bf16),
            pltpu.VMEM((2, NDEV, 8, HALF), f32),
            pltpu.VMEM((HALF, 3 * HALF), bf16),
            pltpu.VMEM((NDEV, 16, HALF), bf16),
            pltpu.VMEM((NORB, K, 16, HALF), bf16),
            pltpu.VMEM((NORB, 8, NT, NT), bf16),
            pltpu.VMEM((9, 2, 8 * HALF, NT), bf16),
            pltpu.VMEM((2, NT, 24 * HALF), bf16),
        ]
        + [dma((4,))] * 6
        + [dma],
        compiler_params=pltpu.CompilerParams(has_side_effects=True, collective_id=0, vmem_limit_bytes=56 << 20),
        cost_estimate=pl.CostEstimate(flops=7 * 10**9, bytes_accessed=2 << 20, transcendentals=0),
    )(planes, bubble_weight)
    return out.reshape(green_packed.shape)


def solution(mesh):
    return jax.shard_map(
        local,
        mesh=mesh,
        in_specs=(P(None, "wide", "orb", None, None), P(), P(), P()),
        out_specs=P(None, "wide", "orb", None, None),
        check_vma=False,
    )
```

time: 108 us -> 96.5 us (0.89)
  Pallas kernels: 106 us -> 94.1 us
    pallas_call x1, Pallas kernels: 106 us -> 94.1 us  [local(): pl.pallas_call(kernel, out_shape=jax.ShapeDtypeStruct((8, NT, NT), bf16),...]
where the time goes in v1:
time: 96.5 us; the launch traced here: 96.4 us
  Pallas kernels  94.1 us (98%)
  local copies, waits for them, and re-layouts  2.26 us (2%)
    pallas_call x1, Pallas kernels, local(): pl.pallas_call(kernel, out_shape=jax.ShapeDtypeStruct((8, NT, NT), bf16),...  94.1 us
    unnamed x1, local copies, waits for them, and re-layouts  2.26 us

profile of v1, /device:TPU:1, one launch (start us, length us, event | category | flops | bytes accessed | tf_op | source)
XLA Modules:
  0.0 96.4 jit_solution(13275059577966311954)
XLA Ops:
  0.0 94.1 %shard_map.28 = bf16[8,256,256]{2,1,0:T(8,128)(2,1)} custom-call(bf16[8,256,256]{2,1,0:T(8,128)(2,1)} %bitcast.5, f32[16,16]{1,0:T(8,128)} %w_ref.1), custom_call_target="tpu_custom_call" | custom-call | flops 7000000000 | bytes 2097152 | tf_op jit(solution)/shard_map/pallas_call | solution.py:352
  94.2 2.3 %copy.5 = bf16[2,1,4,256,256]{4,3,2,1,0:T(8,128)(2,1)} copy(bf16[2,1,4,256,256]{4,3,2,1,0:T(8,128)(2,1)} %bitcast.4) | data formatting | bytes 2097152

commit v2 on v1

--- a/solution.py
+++ b/solution.py
@@ -1,3 +1,4 @@
+import functools
 import math
 
 import jax
@@ -12,11 +13,15 @@
 K = 64
 HALF = 128
 NDEV = 256
+STEP = 264
+ORDER = (2, 1, 3, 0)
+FIRST = {0: 4}
+SECOND = {4: 2}
 
 f32 = jnp.float32
 bf16 = jnp.bfloat16
 
-R00, R11, R10, L00, L11, L01, A00, A11, A01 = range(9)
+R10, R00, R11, A00, L00, A01, L01, A11, L11 = range(9)
 
 
 def shear(x, h):
@@ -111,23 +116,27 @@
 
     barrier = pltpu.get_barrier_semaphore()
 
-    def greet(i, carry):
+    def greet(i):
         pl.semaphore_signal(barrier, inc=1, device_id=place((me + i) % NDEV), device_id_type=pl.DeviceIdType.MESH)
-        return carry
-
-    lax.fori_loop(1, NDEV, greet, 0)
+
+    for i in range(249, 256):
+        greet(i)
 
     def shear_plane(p, carry):
+        for n in range(32):
+            if n < 31:
+                greet(p * 31 + n + 1)
+
         c, b = p // 4, p % 4
         for h in range(2):
             x = x_ref[p, :, h * HALF : (h + 1) * HALF].astype(f32)
-            rows[pl.ds(pl.multiple_of((c * 8 + h * 4 + b) * NT, NT), NT), :] = shear(x, h)
+            rows[pl.ds(pl.multiple_of((c * 8 + h * 4 + b) * STEP, 8), NT), :] = shear(x, h)
         return carry
 
     lax.fori_loop(0, 8, shear_plane, 0)
 
     def make_tile(e):
-        snd[e] = tile_of((rows[pl.ds(e, 8, stride=NT), :], rows[pl.ds(8 * NT + e, 8, stride=NT), :]))
+        snd[e] = tile_of((rows[pl.ds(e, 8, stride=STEP), :], rows[pl.ds(8 * STEP + e, 8, stride=STEP), :]))
 
     def pack(i, carry):
         for n in range(4):
@@ -138,23 +147,38 @@
     rcv[orb, wide] = snd[me]
     pl.semaphore_wait(barrier, NDEV - 1)
 
-    def send(i, carry):
-        step, n = i // K, i % K
+    def send(step, i, carry):
+        n = i % K
         there = (wide + n) % K
         plane = (orb + step) % NORB
         d = there * NORB + plane
         pltpu.make_async_remote_copy(snd.at[d], rcv.at[orb, wide], s1.at[step], r1.at[step], device_id=(there, plane)).start()
         return carry
 
-    lax.fori_loop(1, NDEV, send, 0)
+    for step in ORDER:
+        lax.fori_loop(0 if step else 1, K, functools.partial(send, step), 0)
 
     right, left_ = (orb + 1) % NORB, (orb + 3) % NORB
-    hops = [
-        pltpu.make_async_remote_copy(x_ref, g.at[orb], s2.at[0], r2.at[0], device_id=(wide, right)),
-        pltpu.make_async_remote_copy(x_ref, g.at[orb], s2.at[1], r2.at[1], device_id=(wide, left_)),
-    ]
-    for hop in hops:
-        hop.start()
+    started, halves = [], []
+
+    def hop(source, planes, target, n):
+        copy = pltpu.make_async_remote_copy(source, planes, s2.at[n], r2.at[n], device_id=(wide, target))
+        copy.start()
+        return copy
+
+    def gather(when):
+        for _ in range(FIRST.get(when, 0)):
+            n = len(started)
+            up, down = pl.ds(2 * n, 2), pl.ds(6 - 2 * n, 2)
+            started.append((hop(x_ref.at[up], g.at[orb, up], right, n), hop(x_ref.at[down], g.at[orb, down], left_, 4 + n)))
+        for _ in range(SECOND.get(when, 0)):
+            n = len(halves)
+            up, down = pl.ds(2 * n, 2), pl.ds(6 - 2 * n, 2)
+            for copy in started[n]:
+                copy.wait_recv()
+            halves.append((hop(g.at[left_, up], g.at[left_, up], right, 8 + n), hop(g.at[right, down], g.at[right, down], left_, 10 + n)))
+
+    gather(0)
     own = pltpu.make_async_copy(x_ref, g.at[orb], s4)
     own.start()
 
@@ -172,69 +196,63 @@
         wide_w.append(jnp.where(same, z, 0.0).astype(bf16))
     wv[...] = jnp.concatenate([wide_w[0], wide_w[1], wide_w[0]], axis=1)
 
+    low = me % HALF
+    perm = jnp.where(i0 == (i1 ^ low), 1.0, 0.0).astype(bf16)
+
     arrived = []
-    for step in range(NORB):
+    for step in ORDER:
         a = (orb + NORB - step) % NORB
         count = K - 1 if step == 0 else K
         block = rcv.at[0, pl.ds(0, count)]
         arrived.append(pltpu.make_async_remote_copy(block, block, s1.at[step], r1.at[step], device_id=(wide, orb)))
-        arrived[step].wait_recv()
+        arrived[-1].wait_recv()
 
         def store(r, v):
-            rg[r * NORB + a] = tile_of(v)
+            rg[a, r] = tile_of(v)
 
         fft64(lambda k: both_parts(rcv[a, k]), store, mid, 1)
-
-    for hop in hops:
-        hop.wait_recv()
-    more = [
-        pltpu.make_async_remote_copy(g.at[left_, pl.ds(0, 4)], g.at[left_, pl.ds(0, 4)], s2.at[2], r2.at[2], device_id=(wide, right)),
-        pltpu.make_async_remote_copy(g.at[right, pl.ds(4, 4)], g.at[right, pl.ds(4, 4)], s2.at[3], r2.at[3], device_id=(wide, left_)),
-    ]
-    for hop in more:
-        hop.start()
-
-    low = me % HALF
-    perm = jnp.where(i0 == (i1 ^ low), 1.0, 0.0).astype(bf16)
-
-    def mirror_rows(i, carry):
-        block = rg[pl.ds(i * 32, 32)].reshape(512, HALF)
-        out = jnp.dot(block, perm, preferred_element_type=f32)
-        mir[pl.ds(i * 32, 32)] = out.astype(bf16).reshape(32, 16, HALF)
-        return carry
-
-    lax.fori_loop(0, 8, mirror_rows, 0)
+        gather(len(arrived))
+        for n in range(2):
+            block = rg[a, n * 32 : (n + 1) * 32].reshape(32 * 16, HALF)
+            out = jnp.dot(block, perm, preferred_element_type=f32)
+            mir[a, n * 32 : (n + 1) * 32] = out.astype(bf16).reshape(32, 16, HALF)
 
     swap = (lax.broadcasted_iota(jnp.int32, (8, HALF), 0) * 0 + me // HALF) == 1
 
-    def sites(i, carry):
-        prod_re, prod_im = [], []
+    def four_sites(first):
+        prod_re, prod_im, owns = [], [], []
         for n in range(4):
-            r = i * 4 + n
+            r = first + n
             back = (K - r) % K
             for a in range(4):
-                u = both_parts(rg[r * NORB + a])
-                v = both_parts(mir[back * NORB + a])
+                u = both_parts(rg[a, r])
+                v = both_parts(mir[a, back])
                 v = tuple(jnp.where(swap, pltpu.roll(z, 4, 0), z) for z in v)
                 prod_re.append(u[0] * v[0] - u[1] * v[1])
                 prod_im.append(u[0] * v[1] + u[1] * v[0])
         prod = jnp.concatenate([jnp.concatenate(prod_re, axis=0), jnp.concatenate(prod_im, axis=0)], axis=1)
         high = prod.astype(bf16)
         rest = (prod - high.astype(f32)).astype(bf16)
-        bubble = jnp.dot(wv[...], jnp.concatenate([high, high, rest], axis=0), preferred_element_type=f32)
-        for n in range(4):
-            r = i * 4 + n
-            for a in range(4):
-                row = (n * 4 + a) * 8
-                re, im = bubble[row : row + 8, :HALF], bubble[row : row + 8, HALF:]
-                u = both_parts(rg[r * NORB + a])
-                self_real[0, r * NORB + a] = u[0] * re - u[1] * im
-                self_real[1, r * NORB + a] = u[0] * im + u[1] * re
-        return carry
-
-    lax.fori_loop(0, K // 4, sites, 0)
-
-    for step in range(NORB):
+        return jnp.dot(wv[...], jnp.concatenate([high, high, rest], axis=0), preferred_element_type=f32)
+
+    def sites(i, carry):
+        bubbles = [four_sites(i * 16 + m * 4) for m in range(4)]
+        for m in range(4):
+            for n in range(4):
+                r = i * 16 + m * 4 + n
+                for a in range(4):
+                    row = (n * 4 + a) * 8
+                    re, im = bubbles[m][row : row + 8, :HALF], bubbles[m][row : row + 8, HALF:]
+                    u = both_parts(rg[a, r])
+                    self_real[0, r * NORB + a] = u[0] * re - u[1] * im
+                    self_real[1, r * NORB + a] = u[0] * im + u[1] * re
+        return carry
+
+    lax.fori_loop(0, K // 16, sites, 0)
+
+    gather(5)
+
+    for turn_n, step in enumerate(ORDER):
         a = (orb + step) % NORB
 
         def store(k, v):
@@ -250,11 +268,12 @@
             return carry
 
         lax.fori_loop(1 if step == 0 else 0, K, send_back, 0)
+        gather(6 + turn_n)
     rcv2[orb, wide] = snd2[me]
 
     own.wait()
-    for hop in more:
-        hop.wait_recv()
+    for copy in sum(started[2:] + halves, ()):
+        copy.wait_recv()
     ge, gt = i0 >= i1, i0 > i1
 
     def operands(i, carry):
@@ -263,7 +282,9 @@
             b = bp * 2 + half
             lanes = slice(half * HALF, (half + 1) * HALF)
             for part in range(2):
-                m = pl.ds(pl.multiple_of((c * 2 + part) * HALF, HALF), HALF)
+                def m(block):
+                    return pl.ds(pl.multiple_of(block * 8 * HALF + (c * 2 + part) * HALF, HALF), HALF)
+
                 own_g = g[c, part * 4 + b].astype(f32)
                 adjoint = g[b, part * 4 + c].astype(f32).T
                 if part:
@@ -271,22 +292,22 @@
                 for n in range(2):
                     blk = slice(n * HALF, (n + 1) * HALF)
                     x, y = own_g[blk, blk], adjoint[blk, blk]
-                    rhs[R00 + n, bp, m, lanes] = jnp.where(ge, x, 0.0).astype(bf16)
-                    rhs[L00 + n, bp, m, lanes] = jnp.where(ge, jnp.where(gt, -y, 0.0), x).astype(bf16)
-                    rhs[A00 + n, bp, m, lanes] = jnp.where(gt, 0.0, y).astype(bf16)
-                rhs[R10, bp, m, lanes] = own_g[HALF:, :HALF].astype(bf16)
-                rhs[L01, bp, m, lanes] = own_g[:HALF, HALF:].astype(bf16)
-                rhs[A01, bp, m, lanes] = adjoint[:HALF, HALF:].astype(bf16)
+                    rhs[bp, m((R00, R11)[n]), lanes] = jnp.where(ge, x, 0.0).astype(bf16)
+                    rhs[bp, m((L00, L11)[n]), lanes] = jnp.where(ge, jnp.where(gt, -y, 0.0), x).astype(bf16)
+                    rhs[bp, m((A00, A11)[n]), lanes] = jnp.where(gt, 0.0, y).astype(bf16)
+                rhs[bp, m(R10), lanes] = own_g[HALF:, :HALF].astype(bf16)
+                rhs[bp, m(L01), lanes] = own_g[:HALF, HALF:].astype(bf16)
+                rhs[bp, m(A01), lanes] = adjoint[:HALF, HALF:].astype(bf16)
         return carry
 
     lax.fori_loop(0, 8, operands, 0)
 
     returned = []
-    for step in range(NORB):
+    for step in ORDER:
         count = K - 1 if step == 0 else K
         block = rcv2.at[0, pl.ds(0, count)]
         returned.append(pltpu.make_async_remote_copy(block, block, s3.at[step], r3.at[step], device_id=(wide, orb)))
-        returned[step].wait_recv()
+        returned[-1].wait_recv()
         plane = (orb + NORB - step) % NORB
 
         def spread(i, carry):
@@ -294,8 +315,8 @@
                 w = i * 4 + n
                 e = w * NORB + plane
                 re, im = both_parts(rcv2[plane, w])
-                rows[pl.ds(e, 8, stride=NT), :] = re
-                rows[pl.ds(8 * NT + e, 8, stride=NT), :] = im
+                rows[pl.ds(e, 8, stride=STEP), :] = re
+                rows[pl.ds(8 * STEP + e, 8, stride=STEP), :] = im
             return carry
 
         lax.fori_loop(0, K // 4, spread, 0)
@@ -303,12 +324,12 @@
     def left(c, carry):
         for h in range(2):
             for part in range(2):
-                x = shear(rows[pl.ds(pl.multiple_of((part * 8 + h * 4 + c) * NT, NT), NT), :], h)
+                x = shear(rows[pl.ds(pl.multiple_of((part * 8 + h * 4 + c) * STEP, 8), NT), :], h)
                 top, low_half = x[:HALF], x[HALF:]
                 if h == 0:
-                    placed = ((0, 0, jnp.where(ge, top, 0.0)), (0, 1, jnp.where(ge, 0.0, top)), (1, 0, low_half))
+                    placed = ((0, 1, jnp.where(ge, top, 0.0)), (0, 0, jnp.where(ge, 0.0, top)), (1, 0, low_half), (1, 3, low_half))
                 else:
-                    placed = ((0, 2, top), (1, 1, jnp.where(ge, low_half, 0.0)), (1, 2, jnp.where(ge, 0.0, low_half)))
+                    placed = ((0, 2, top), (1, 2, jnp.where(ge, low_half, 0.0)), (1, 1, jnp.where(ge, 0.0, low_half)))
                 for t, n, z in placed:
                     same = pl.multiple_of(n * 8 * HALF + (c * 2 + part) * HALF, HALF)
                     other = pl.multiple_of(n * 8 * HALF + (c * 2 + 1 - part) * HALF, HALF)
@@ -319,19 +340,19 @@
     lax.fori_loop(0, NORB, left, 0)
 
     def products(bp, carry):
-        def dot(t, first, *blocks):
-            z = lhs[t, :, first * 8 * HALF : (first + len(blocks)) * 8 * HALF]
-            return jnp.dot(z, jnp.concatenate([rhs[n, bp] for n in blocks], axis=0), preferred_element_type=f32)
+        def dot(t, first, block, count=1):
+            z = lhs[t, :, first * 8 * HALF : (first + count) * 8 * HALF]
+            return jnp.dot(z, rhs[bp, block * 8 * HALF : (block + count) * 8 * HALF], preferred_element_type=f32)
 
         mask = jnp.concatenate([jnp.concatenate([ge, ge], axis=0)] * 2, axis=1)
         quarters = {
-            (0, 0): jnp.where(mask, dot(0, 0, R00), dot(0, 0, L00, A00)),
-            (0, 1): dot(0, 0, L01, A01, A11),
-            (1, 0): dot(1, 0, R00, R10),
-            (1, 1): jnp.where(mask, dot(1, 1, R11), dot(1, 0, L01, L11, A11)),
+            (0, 0): jnp.where(mask, dot(0, 1, R00), dot(0, 0, A00, 2)),
+            (0, 1): dot(0, 0, A01, 3),
+            (1, 0): dot(1, 2, R10, 2),
+            (1, 1): jnp.where(mask, dot(1, 2, R11), dot(1, 0, L01, 3)),
         }
         for (t, u), z in quarters.items():
-            z = (z * NT ** (-0.5)).astype(bf16)
+            z = z.astype(bf16)
             for part in range(2):
                 for half in range(2):
                     o_ref[part * 4 + bp * 2 + half, t * HALF : (t + 1) * HALF, u * HALF : (u + 1) * HALF] = z[
@@ -341,7 +362,7 @@
 
     lax.fori_loop(0, 2, products, 0)
 
-    for copy in arrived + hops + more + returned:
+    for copy in arrived + list(sum(started + halves, ())) + returned:
         copy.wait_send()
 
 
@@ -355,26 +376,28 @@
         in_specs=[vmem, vmem],
         out_specs=vmem,
         scratch_shapes=[
-            pltpu.VMEM((16 * NT, HALF), f32),
+            pltpu.VMEM((16 * STEP, HALF), f32),
             pltpu.VMEM((NDEV, 16, HALF), bf16),
             pltpu.VMEM((NORB, K, 16, HALF), bf16),
             pltpu.VMEM((2, K, 8, HALF), f32),
-            pltpu.VMEM((NDEV, 16, HALF), bf16),
-            pltpu.VMEM((NDEV, 16, HALF), bf16),
+            pltpu.VMEM((NORB, K, 16, HALF), bf16),
+            pltpu.VMEM((NORB, K, 16, HALF), bf16),
             pltpu.VMEM((2, NDEV, 8, HALF), f32),
             pltpu.VMEM((HALF, 3 * HALF), bf16),
             pltpu.VMEM((NDEV, 16, HALF), bf16),
             pltpu.VMEM((NORB, K, 16, HALF), bf16),
             pltpu.VMEM((NORB, 8, NT, NT), bf16),
-            pltpu.VMEM((9, 2, 8 * HALF, NT), bf16),
-            pltpu.VMEM((2, NT, 24 * HALF), bf16),
+            pltpu.VMEM((2, 72 * HALF, NT), bf16),
+            pltpu.VMEM((2, NT, 32 * HALF), bf16),
         ]
-        + [dma((4,))] * 6
+        + [dma((4,))] * 2
+        + [dma((12,))] * 2
+        + [dma((4,))] * 2
         + [dma],
         compiler_params=pltpu.CompilerParams(has_side_effects=True, collective_id=0, vmem_limit_bytes=56 << 20),
         cost_estimate=pl.CostEstimate(flops=7 * 10**9, bytes_accessed=2 << 20, transcendentals=0),
     )(planes, bubble_weight)
-    return out.reshape(green_packed.shape)
+    return out.reshape(green_packed.shape) * jnp.asarray(NT ** (-0.5), bf16)
 
 
 def solution(mesh):

time: 96.5 us -> 87.7 us (0.909)
  Pallas kernels: 94.1 us -> 85.3 us
  other arithmetic: 0 us -> 2.29 us
  local copies, waits for them, and re-layouts: 2.26 us -> 0 us
    pallas_call x1, Pallas kernels: 94.1 us -> 85.3 us  [local(): pl.pallas_call(kernel, out_shape=jax.ShapeDtypeStruct((8, NT, NT), bf16),...]
    mul x0 -> x1, other arithmetic: none -> 2.29 us  [local(): return out.reshape(green_packed.shape) * jnp.asarray(NT ** (-0.5), bf16)]
    unnamed x1 -> x0, local copies, waits for them, and re-layouts: 2.26 us -> none
where the time goes in v2:
time: 87.7 us; the launch traced here: 87.6 us
  Pallas kernels  85.3 us (97%)
  other arithmetic  2.29 us (3%)
    pallas_call x1, Pallas kernels, local(): pl.pallas_call(kernel, out_shape=jax.ShapeDtypeStruct((8, NT, NT), bf16),...  85.3 us
    mul x1, other arithmetic, local(): return out.reshape(green_packed.shape) * jnp.asarray(NT ** (-0.5), bf16)  2.29 us

profile of v2, /device:TPU:1, one launch (start us, length us, event | category | flops | bytes accessed | tf_op | source)
XLA Modules:
  0.0 87.6 jit_solution(17827138729632706557)
XLA Ops:
  0.0 85.3 %shard_map.28 = bf16[8,256,256]{2,1,0:T(8,128)(2,1)} custom-call(bf16[8,256,256]{2,1,0:T(8,128)(2,1)} %bitcast.4, f32[16,16]{1,0:T(8,128)} %w_ref.1), custom_call_target="tpu_custom_call" | custom-call | flops 7000000000 | bytes 2097152 | tf_op jit(solution)/shard_map/pallas_call | solution.py:373
  85.3 2.3 %broadcast_multiply_fusion = bf16[8,256,256]{2,1,0:T(8,128)(2,1)} fusion(bf16[8,256,256]{2,1,0:T(8,128)(2,1)} %shard_map.28), kind=kLoop, calls=%fused_computation | loop fusion | flops 524288 | bytes 2097152 | tf_op jit(solution)/shard_map/mul | solution.py:400

commit v3 on v2

--- a/solution.py
+++ b/solution.py
@@ -394,7 +394,7 @@
         + [dma((12,))] * 2
         + [dma((4,))] * 2
         + [dma],
-        compiler_params=pltpu.CompilerParams(has_side_effects=True, collective_id=0, vmem_limit_bytes=56 << 20),
+        compiler_params=pltpu.CompilerParams(has_side_effects=True, collective_id=0, vmem_limit_bytes=38 << 20),
         cost_estimate=pl.CostEstimate(flops=7 * 10**9, bytes_accessed=2 << 20, transcendentals=0),
     )(planes, bubble_weight)
     return out.reshape(green_packed.shape) * jnp.asarray(NT ** (-0.5), bf16)

time: 87.7 us -> 86.2 us (0.983)
  Pallas kernels: 85.3 us -> 83.1 us
  local copies, waits for them, and re-layouts: 0 us -> 1.92 us
  other arithmetic: 2.29 us -> 1.06 us
    pallas_call x1, Pallas kernels: 85.3 us -> 83.1 us  [local(): pl.pallas_call(kernel, out_shape=jax.ShapeDtypeStruct((8, NT, NT), bf16),...]
    unnamed x0 -> x4, local copies, waits for them, and re-layouts: none -> 1.92 us
    mul x1, other arithmetic: 2.29 us -> 1.06 us  [local(): return out.reshape(green_packed.shape) * jnp.asarray(NT ** (-0.5), bf16)]
where the time goes in v3:
time: 86.2 us; the launch traced here: 86.1 us
  Pallas kernels  83.1 us (96%)
  local copies, waits for them, and re-layouts  1.92 us (2%)
  other arithmetic  1.06 us (1%)
    pallas_call x1, Pallas kernels, local(): pl.pallas_call(kernel, out_shape=jax.ShapeDtypeStruct((8, NT, NT), bf16),...  83.1 us
    unnamed x4, local copies, waits for them, and re-layouts  1.92 us

profile of v3, /device:TPU:1, one launch (start us, length us, event | category | flops | bytes accessed | tf_op | source)
XLA Modules:
  0.0 86.1 jit_solution(8696721627948142393)
XLA Ops:
  0.0 0.0 copy-start
  0.0 1.2 %copy-done = bf16[2,1,4,256,256]{4,3,2,1,0:T(8,128)(2,1)S(1)} copy-done((bf16[2,1,4,256,256]{4,3,2,1,0:T(8,128)(2,1)S(1)}, bf16[2,1,4,256,256]{4,3,2,1,0:T(8,128)(2,1)}, u32[]{:S(2)}) %copy-start) | copy-done | bytes 1048600
  1.2 0.0 copy-start.1
  1.2 0.7 copy-done.1
  1.9 83.1 %shard_map.28 = bf16[8,256,256]{2,1,0:T(8,128)(2,1)S(1)} custom-call(bf16[8,256,256]{2,1,0:T(8,128)(2,1)S(1)} %bitcast.4, f32[16,16]{1,0:T(8,128)S(1)} %copy-done.1), custom_call_target="tpu_custom_call" | custom-call | flops 7000000000 | bytes 2097152 | tf_op jit(solution)/shard_map/pallas_call | solution.py:373
  85.0 1.1 %broadcast_multiply_fusion = bf16[8,256,256]{2,1,0:T(8,128)(2,1)} fusion(bf16[8,256,256]{2,1,0:T(8,128)(2,1)S(1)} %shard_map.28), kind=kLoop, calls=%fused_computation | loop fusion | flops 524288 | bytes 2097152 | tf_op jit(solution)/shard_map/mul | solution.py:400
Async XLA Ops:
  0.0 1.2 %copy-start = (bf16[2,1,4,256,256]{4,3,2,1,0:T(8,128)(2,1)S(1)}, bf16[2,1,4,256,256]{4,3,2,1,0:T(8,128)(2,1)}, u32[]{:S(2)}) copy-start(bf16[2,1,4,256,256]{4,3,2,1,0:T(8,128)(2,1)} %param.4) | copy-start | bytes 3145732
  1.2 0.7 copy-start.1

commit v4 on v3

--- a/solution.py
+++ b/solution.py
@@ -115,17 +115,21 @@
         return (d // NORB, d % NORB)
 
     barrier = pltpu.get_barrier_semaphore()
-
-    def greet(i):
-        pl.semaphore_signal(barrier, inc=1, device_id=place((me + i) % NDEV), device_id_type=pl.DeviceIdType.MESH)
-
-    for i in range(249, 256):
-        greet(i)
+    planes = [lax.rem(orb + step, NORB) for step in range(NORB)]
 
     def shear_plane(p, carry):
-        for n in range(32):
-            if n < 31:
-                greet(p * 31 + n + 1)
+        for n in range(8):
+            there = lax.rem(wide + p * 8 + n, K)
+            for step in range(NORB):
+
+                def greet(there=there, step=step):
+                    device = (there, planes[step])
+                    pl.semaphore_signal(barrier, inc=1, device_id=device, device_id_type=pl.DeviceIdType.MESH)
+
+                if n or step:
+                    greet()
+                else:
+                    pl.when(p > 0)(greet)
 
         c, b = p // 4, p % 4
         for h in range(2):
@@ -148,9 +152,8 @@
     pl.semaphore_wait(barrier, NDEV - 1)
 
     def send(step, i, carry):
-        n = i % K
-        there = (wide + n) % K
-        plane = (orb + step) % NORB
+        there = lax.rem(wide + i, K)
+        plane = planes[step]
         d = there * NORB + plane
         pltpu.make_async_remote_copy(snd.at[d], rcv.at[orb, wide], s1.at[step], r1.at[step], device_id=(there, plane)).start()
         return carry
@@ -261,7 +264,7 @@
         fft64(lambda r: (self_real[0, r * NORB + a], self_real[1, r * NORB + a]), store, mid, -1)
 
         def send_back(n, carry):
-            k = (wide + n) % K
+            k = lax.rem(wide + n, K)
             pltpu.make_async_remote_copy(
                 snd2.at[k * NORB + a], rcv2.at[orb, wide], s3.at[step], r3.at[step], device_id=(k, a)
             ).start()

time: 86.2 us -> 84.4 us (0.979)
  Pallas kernels: 83.1 us -> 81.3 us
    pallas_call x1, Pallas kernels: 83.1 us -> 81.3 us  [local(): pl.pallas_call(kernel, out_shape=jax.ShapeDtypeStruct((8, NT, NT), bf16),...]
where the time goes in v4:
time: 84.4 us; the launch traced here: 84.3 us
  Pallas kernels  81.3 us (96%)
  local copies, waits for them, and re-layouts  1.92 us (2%)
  other arithmetic  1.06 us (1%)
    pallas_call x1, Pallas kernels, local(): pl.pallas_call(kernel, out_shape=jax.ShapeDtypeStruct((8, NT, NT), bf16),...  81.3 us
    unnamed x4, local copies, waits for them, and re-layouts  1.92 us

profile of v4, /device:TPU:1, one launch (start us, length us, event | category | flops | bytes accessed | tf_op | source)
XLA Modules:
  0.0 84.3 jit_solution(11635123080998660952)
XLA Ops:
  0.0 0.0 copy-start
  0.0 1.2 %copy-done = bf16[2,1,4,256,256]{4,3,2,1,0:T(8,128)(2,1)S(1)} copy-done((bf16[2,1,4,256,256]{4,3,2,1,0:T(8,128)(2,1)S(1)}, bf16[2,1,4,256,256]{4,3,2,1,0:T(8,128)(2,1)}, u32[]{:S(2)}) %copy-start) | copy-done | bytes 1048600
  1.2 0.0 copy-start.1
  1.2 0.7 copy-done.1
  1.9 81.3 %shard_map.28 = bf16[8,256,256]{2,1,0:T(8,128)(2,1)S(1)} custom-call(bf16[8,256,256]{2,1,0:T(8,128)(2,1)S(1)} %bitcast.4, f32[16,16]{1,0:T(8,128)S(1)} %copy-done.1), custom_call_target="tpu_custom_call" | custom-call | flops 7000000000 | bytes 2097152 | tf_op jit(solution)/shard_map/pallas_call | solution.py:376
  83.2 1.1 %broadcast_multiply_fusion = bf16[8,256,256]{2,1,0:T(8,128)(2,1)} fusion(bf16[8,256,256]{2,1,0:T(8,128)(2,1)S(1)} %shard_map.28), kind=kLoop, calls=%fused_computation | loop fusion | flops 524288 | bytes 2097152 | tf_op jit(solution)/shard_map/mul | solution.py:403
Async XLA Ops:
  0.0 1.2 %copy-start = (bf16[2,1,4,256,256]{4,3,2,1,0:T(8,128)(2,1)S(1)}, bf16[2,1,4,256,256]{4,3,2,1,0:T(8,128)(2,1)}, u32[]{:S(2)}) copy-start(bf16[2,1,4,256,256]{4,3,2,1,0:T(8,128)(2,1)} %param.4) | copy-start | bytes 3145732
  1.2 0.7 copy-start.1

commit v5 on v4

--- a/solution.py
+++ b/solution.py
@@ -142,14 +142,10 @@
     def make_tile(e):
         snd[e] = tile_of((rows[pl.ds(e, 8, stride=STEP), :], rows[pl.ds(8 * STEP + e, 8, stride=STEP), :]))
 
-    def pack(i, carry):
-        for n in range(4):
-            make_tile(i * 4 + n)
-        return carry
-
-    lax.fori_loop(0, NDEV // 4, pack, 0)
-    rcv[orb, wide] = snd[me]
-    pl.semaphore_wait(barrier, NDEV - 1)
+    def pack(step, i, carry):
+        for n in range(8):
+            make_tile((i * 8 + n) * NORB + planes[step])
+        return carry
 
     def send(step, i, carry):
         there = lax.rem(wide + i, K)
@@ -159,7 +155,11 @@
         return carry
 
     for step in ORDER:
+        lax.fori_loop(0, K // 8, functools.partial(pack, step), 0)
+        if step == ORDER[0]:
+            pl.semaphore_wait(barrier, NDEV - 1)
         lax.fori_loop(0 if step else 1, K, functools.partial(send, step), 0)
+    rcv[orb, wide] = snd[me]
 
     right, left_ = (orb + 1) % NORB, (orb + 3) % NORB
     started, halves = [], []
@@ -251,7 +251,7 @@
                     self_real[1, r * NORB + a] = u[0] * im + u[1] * re
         return carry
 
-    lax.fori_loop(0, K // 16, sites, 0)
+    lax.fori_loop(0, K // 16, sites, 0, unroll=True)
 
     gather(5)
 
@@ -340,7 +340,7 @@
                     lhs[t, HALF:, pl.ds(other, HALF)] = z.astype(bf16)
         return carry
 
-    lax.fori_loop(0, NORB, left, 0)
+    lax.fori_loop(0, NORB, left, 0, unroll=True)
 
     def products(bp, carry):
         def dot(t, first, block, count=1):
@@ -363,7 +363,7 @@
                     ]
         return carry
 
-    lax.fori_loop(0, 2, products, 0)
+    lax.fori_loop(0, 2, products, 0, unroll=True)
 
     for copy in arrived + list(sum(started + halves, ())) + returned:
         copy.wait_send()

time: 84.4 us -> 83.6 us (level)
  no operation moved by 1% of the time
where the time goes in v5:
time: 83.6 us; the launch traced here: 83.5 us
  Pallas kernels  80.5 us (96%)
  local copies, waits for them, and re-layouts  1.92 us (2%)
  other arithmetic  1.06 us (1%)
    pallas_call x1, Pallas kernels, local(): pl.pallas_call(kernel, out_shape=jax.ShapeDtypeStruct((8, NT, NT), bf16),...  80.5 us
    unnamed x4, local copies, waits for them, and re-layouts  1.92 us

profile of v5, /device:TPU:1, one launch (start us, length us, event | category | flops | bytes accessed | tf_op | source)
XLA Modules:
  0.0 83.5 jit_solution(18107144577679083604)
XLA Ops:
  0.0 0.0 copy-start
  0.0 1.2 %copy-done = bf16[2,1,4,256,256]{4,3,2,1,0:T(8,128)(2,1)S(1)} copy-done((bf16[2,1,4,256,256]{4,3,2,1,0:T(8,128)(2,1)S(1)}, bf16[2,1,4,256,256]{4,3,2,1,0:T(8,128)(2,1)}, u32[]{:S(2)}) %copy-start) | copy-done | bytes 1048600
  1.2 0.0 copy-start.1
  1.2 0.7 copy-done.1
  1.9 80.5 %shard_map.28 = bf16[8,256,256]{2,1,0:T(8,128)(2,1)S(1)} custom-call(bf16[8,256,256]{2,1,0:T(8,128)(2,1)S(1)} %bitcast.4, f32[16,16]{1,0:T(8,128)S(1)} %copy-done.1), custom_call_target="tpu_custom_call" | custom-call | flops 7000000000 | bytes 2097152 | tf_op jit(solution)/shard_map/pallas_call | solution.py:376
  82.4 1.1 %broadcast_multiply_fusion = bf16[8,256,256]{2,1,0:T(8,128)(2,1)} fusion(bf16[8,256,256]{2,1,0:T(8,128)(2,1)S(1)} %shard_map.28), kind=kLoop, calls=%fused_computation | loop fusion | flops 524288 | bytes 2097152 | tf_op jit(solution)/shard_map/mul | solution.py:403
Async XLA Ops:
  0.0 1.2 %copy-start = (bf16[2,1,4,256,256]{4,3,2,1,0:T(8,128)(2,1)S(1)}, bf16[2,1,4,256,256]{4,3,2,1,0:T(8,128)(2,1)}, u32[]{:S(2)}) copy-start(bf16[2,1,4,256,256]{4,3,2,1,0:T(8,128)(2,1)} %param.4) | copy-start | bytes 3145732
  1.2 0.7 copy-start.1

commit v6 on v5

--- a/solution.py
+++ b/solution.py
@@ -16,7 +16,7 @@
 STEP = 264
 ORDER = (2, 1, 3, 0)
 FIRST = {0: 4}
-SECOND = {4: 2}
+SECOND = {3: 1, 4: 1}
 
 f32 = jnp.float32
 bf16 = jnp.bfloat16

time: 83.6 us -> 83.6 us (level)
  no operation moved by 1% of the time
where the time goes in v6:
time: 83.6 us; the launch traced here: 83.5 us
  Pallas kernels  80.5 us (96%)
  local copies, waits for them, and re-layouts  1.92 us (2%)
  other arithmetic  1.06 us (1%)
    pallas_call x1, Pallas kernels, local(): pl.pallas_call(kernel, out_shape=jax.ShapeDtypeStruct((8, NT, NT), bf16),...  80.5 us
    unnamed x4, local copies, waits for them, and re-layouts  1.92 us

profile of v6, /device:TPU:1, one launch (start us, length us, event | category | flops | bytes accessed | tf_op | source)
XLA Modules:
  0.0 83.5 jit_solution(727846015844867976)
XLA Ops:
  0.0 0.0 copy-start
  0.0 1.2 %copy-done = bf16[2,1,4,256,256]{4,3,2,1,0:T(8,128)(2,1)S(1)} copy-done((bf16[2,1,4,256,256]{4,3,2,1,0:T(8,128)(2,1)S(1)}, bf16[2,1,4,256,256]{4,3,2,1,0:T(8,128)(2,1)}, u32[]{:S(2)}) %copy-start) | copy-done | bytes 1048600
  1.2 0.0 copy-start.1
  1.2 0.7 copy-done.1
  1.9 80.5 %shard_map.28 = bf16[8,256,256]{2,1,0:T(8,128)(2,1)S(1)} custom-call(bf16[8,256,256]{2,1,0:T(8,128)(2,1)S(1)} %bitcast.4, f32[16,16]{1,0:T(8,128)S(1)} %copy-done.1), custom_call_target="tpu_custom_call" | custom-call | flops 7000000000 | bytes 2097152 | tf_op jit(solution)/shard_map/pallas_call | solution.py:376
  82.4 1.1 %broadcast_multiply_fusion = bf16[8,256,256]{2,1,0:T(8,128)(2,1)} fusion(bf16[8,256,256]{2,1,0:T(8,128)(2,1)S(1)} %shard_map.28), kind=kLoop, calls=%fused_computation | loop fusion | flops 524288 | bytes 2097152 | tf_op jit(solution)/shard_map/mul | solution.py:403
Async XLA Ops:
  0.0 1.2 %copy-start = (bf16[2,1,4,256,256]{4,3,2,1,0:T(8,128)(2,1)S(1)}, bf16[2,1,4,256,256]{4,3,2,1,0:T(8,128)(2,1)}, u32[]{:S(2)}) copy-start(bf16[2,1,4,256,256]{4,3,2,1,0:T(8,128)(2,1)} %param.4) | copy-start | bytes 3145732
  1.2 0.7 copy-start.1
